TPU v7x, 256 devices: a whole 4x4x8 slice. The times are simulated.
256 devices in a mesh: row: 8 (over z_lo, x), col: 4 (over z_hi), depth: 8 (over y, core).
Axes of the slice: x: 4, y: 4, z: 8 (z_hi: 4, z_lo: 2; z = z_hi * 2 + z_lo), core: 2. Of those that a mesh axis runs over, the one named last changes fastest.
Arguments:
- tokens: bfloat16 [8192, 5120], P(('row', 'depth'), 'col'), may hold values from -6 to 6
- bucket_ids: int32 [8192], P(('row', 'depth')), may hold values from 0 to 15
- clip_lengths: int32 [64], replicated, may hold values from 1 to 256, 8192 in all
- shift_table: float32 [16, 5120], replicated, may hold values from -3 to 3
- scale_table: float32 [16, 5120], replicated, may hold values from -2.5 to 2.5
- gate_table: float32 [16, 5120], P(None, 'col'), may hold values from 0.5 to 1.5
- w_qkv: bfloat16 [5120, 7680], P('row', 'col'), may hold values from -0.078125 to 0.078125
- q_gain: float32 [2560], P('col'), may hold values from 0.5 to 1.5
- k_gain: float32 [2560], P('col'), may hold values from 0.5 to 1.5
- w_out: bfloat16 [2560, 5120], P('row', 'col'), may hold values from -0.125 to 0.125
Outputs:
- update: bfloat16 [8192, 5120], P(('row', 'depth'), 'col')
Inputs may be any that keep to these rules, and one draw needn't show every extreme that they name: `clip_lengths`: clip lengths in slab order; they sum to 8192.
All inputs are finite; a program needn't handle non-finite values.
Results may differ from a plain program's by a relative error of at most 0.0081.
Values may be sent and summed in bfloat16 or wider, within the bound.
A program may use at most 128 MiB of HBM per device.

v0:
```python
import math

import jax
import jax.numpy as jnp
from jax import lax
from jax.sharding import PartitionSpec as P

HD = 128
FRAME = 128


eps_norm = 1e-06


def clip_places(first_row, row_count, clip_lengths):
    clip_ends = jnp.cumsum(clip_lengths, dtype=jnp.int32)
    token_index = first_row + jnp.arange(row_count, dtype=jnp.int32)
    passed = clip_ends[None, :] <= token_index[:, None]
    clip_number = jnp.sum(passed.astype(jnp.int32), axis=1, dtype=jnp.int32)
    clip_start = jnp.sum(jnp.where(passed, clip_lengths[None, :], 0), axis=1, dtype=jnp.int32)
    return (clip_number, token_index - clip_start)


def layer_norm(values):
    row_mean = jnp.mean(values, axis=-1, keepdims=True)
    centred = values - row_mean
    spread = jnp.mean(centred * centred, axis=-1, keepdims=True)
    return centred * lax.rsqrt(spread + eps_norm)


def head_norm(vectors, gains):
    power = jnp.mean(vectors * vectors, axis=-1, keepdims=True)
    return vectors * lax.rsqrt(power + eps_norm) * gains


def rotary(vectors, position):
    half_width = vectors.shape[-1] // 2
    inverse = 10000.0 ** (-jnp.arange(half_width, dtype=jnp.float32) / half_width)
    angles = position.astype(jnp.float32)[:, None] * inverse[None, :]
    cosine = jnp.cos(angles)[:, None, :]
    sine = jnp.sin(angles)[:, None, :]
    front = vectors[..., :half_width]
    back = vectors[..., half_width:]
    return jnp.concatenate([front * cosine - back * sine, back * cosine + front * sine], axis=-1)


def frame_attention(queries, keys_rot, values_new, clip_number, frame_len):
    tok_rows, heads_here, head_dim = queries.shape
    frames = tok_rows // frame_len
    frame_shape = (frames, frame_len, heads_here, head_dim)
    scores = jnp.einsum(
        "fqhd,fkhd->fhqk",
        queries.reshape(frame_shape),
        keys_rot.reshape(frame_shape),
        preferred_element_type=jnp.float32,
    ) / math.sqrt(head_dim)
    same_clip = clip_number.reshape(frames, frame_len)
    allowed = same_clip[:, None, :, None] == same_clip[:, None, None, :]
    raised = jnp.where(allowed, jnp.exp(scores), 0.0)
    weights = (raised / jnp.sum(raised, axis=-1, keepdims=True)).astype(jnp.bfloat16)
    attended = jnp.einsum(
        "fhqk,fkhd->fqhd",
        weights,
        values_new.reshape(frame_shape),
        preferred_element_type=jnp.float32,
    )
    return attended.reshape(tok_rows, heads_here * head_dim).astype(jnp.bfloat16)


def add_panel(left_side, panel):
    return jnp.dot(left_side, panel, preferred_element_type=jnp.float32)


def shards(
    tokens,
    bucket_ids,
    clip_lengths,
    shift_table,
    scale_table,
    gate_table,
    w_qkv,
    q_gain,
    k_gain,
    w_out,
):
    tok_rows = tokens.shape[0]
    features = lax.all_gather(tokens, "col", axis=1, tiled=True)
    first_row = lax.axis_index(("row", "depth")) * tok_rows
    clip_number, position = clip_places(first_row, tok_rows, clip_lengths)
    one_hot = (
        bucket_ids[:, None] == jnp.arange(shift_table.shape[0], dtype=jnp.int32)[None, :]
    ).astype(jnp.float32)
    row_shift = jnp.dot(one_hot, shift_table, precision=lax.Precision.HIGHEST)
    row_scale = jnp.dot(one_hot, scale_table, precision=lax.Precision.HIGHEST)
    row_gate = jnp.dot(one_hot, gate_table, precision=lax.Precision.HIGHEST)
    modulated = (layer_norm(features.astype(jnp.float32)) * (1.0 + row_scale) + row_shift).astype(
        jnp.bfloat16
    )
    block_width = w_qkv.shape[1]
    joined = add_panel(modulated, lax.all_gather(w_qkv, "row", axis=0, tiled=True))
    heads_here = block_width // (3 * HD)
    joined = joined.reshape(tok_rows, heads_here, 3, HD)
    queries = rotary(head_norm(joined[:, :, 0], q_gain.reshape(heads_here, HD)), position).astype(
        jnp.bfloat16
    )
    keys_rot = rotary(head_norm(joined[:, :, 1], k_gain.reshape(heads_here, HD)), position).astype(
        jnp.bfloat16
    )
    values_new = joined[:, :, 2].astype(jnp.bfloat16)
    attended = frame_attention(queries, keys_rot, values_new, clip_number, FRAME)
    all_heads = lax.all_gather(attended, "col", axis=1, tiled=True)
    projected = add_panel(all_heads, lax.all_gather(w_out, "row", axis=0, tiled=True))
    return (row_gate * projected).astype(jnp.bfloat16)


def solution(mesh):
    in_specs = (
        P(("row", "depth"), "col"),
        P(("row", "depth")),
        P(),
        P(),
        P(),
        P(None, "col"),
        P("row", "col"),
        P("col"),
        P("col"),
        P("row", "col"),
    )
    out_specs = P(("row", "depth"), "col")
    return jax.shard_map(shards, mesh=mesh, in_specs=in_specs, out_specs=out_specs, check_vma=False)
```

profile of v0, /device:TPU:24, one launch (start us, length us, event | category | flops | bytes accessed | tf_op | source)
XLA Modules:
  0.0 350.5 jit_solution(6082703713997648647)
XLA Ops:
  6.5 0.0 copy-start
  6.5 0.0 copy-start.7
  6.5 0.0 copy-start.4
  6.5 0.0 copy-start.3
  6.5 0.0 all-gather.4.cloned.1.call-start
  6.6 0.7 all-gather.4.cloned.1.call-update
  7.3 0.0 all-gather.6.cloned.1.call-start
  7.3 0.7 all-gather.6.cloned.1.call-update
  8.0 0.0 all-gather.8.cloned.1.call-start
  8.1 0.7 all-gather.8.cloned.1.call-update
  8.8 0.0 copy-done.7
  8.8 0.1 copy.24
  8.9 0.1 reduce-window.8
  9.0 0.1 reduce.2
  9.1 0.1 fusion.28
  9.2 0.1 broadcast_compare_fusion
  9.3 0.3 multiply_cosine_fusion
  9.6 0.0 copy-done.4
  9.6 0.0 copy-done.3
  9.6 0.5 fusion.22
  10.1 40.7 %all-gather.4.cloned.1.call-done = bf16[128,5120]{1,0:T(8,128)(2,1)} async-done(((bf16[128,1280]{1,0:T(8,128)(2,1)}), bf16[128,5120]{1,0:T(8,128)(2,1)}) %all-gather.4.cloned.1.call-update) | async-done | bytes 1310736 | tf_op jit(solution)/shard_map/all_gather | solution.py:87
  50.8 0.0 copy-start.1
  50.8 1.7 convert_reduce_fusion
  52.5 0.0 copy-start.2
  52.5 1.9 fusion.4
  54.3 0.0 copy-done
  54.4 0.0 copy-done.1
  54.4 1.5 fusion
  55.9 0.0 copy-done.2
  55.9 1.4 fusion.1
  57.2 193.6 %all-gather.6.cloned.1.call-done = bf16[5120,1920]{1,0:T(8,128)(2,1)} async-done(((bf16[640,1920]{1,0:T(8,128)(2,1)}), bf16[5120,1920]{1,0:T(8,128)(2,1)}) %all-gather.6.cloned.1.call-update) | async-done | bytes 19660816 | tf_op jit(solution)/shard_map/all_gather | solution.py:100
  250.8 11.7 %fusion.40 = f32[128,1920]{0,1:T(8,128)S(1)} fusion(bf16[128,5120]{1,0:T(8,128)(2,1)S(1)} %fusion.1, bf16[5120,1920]{1,0:T(8,128)(2,1)} %all-gather.6.cloned.1.call-done), kind=kOutput, calls=%fused_computation.63 | convolution fusion | flops 2516582400 | bytes 21954560 | tf_op jit(solution)/shard_map/dot_general | solution.py:71
  262.5 0.0 copy-start.5
  262.6 0.0 copy-start.6
  262.6 0.2 copy.31
  262.8 0.2 copy.30
  263.0 0.2 fusion.8
  263.1 0.2 fusion.10
  263.3 0.0 copy-done.5
  263.3 0.0 copy-done.6
  263.4 0.2 fusion.9
  263.6 0.3 subtract_convert_fusion
  263.9 0.3 fusion.7
  264.2 0.2 convolution_convert_fusion
  264.5 23.1 %all_gather.14 = bf16[128,2560]{0,1:T(8,128)(2,1)S(1)} all-gather(bf16[128,640]{0,1:T(8,128)(2,1)S(1)} %bitcast.36), channel_id=1, replica_groups=mesh['row'=8,'col'=4,'depth'=8] {'col'}, dimensions={1}, use_global_device_ids=true | all-gather | bytes 819200 | tf_op jit(solution)/shard_map/all_gather | solution.py:111
  287.5 51.7 %all-gather.8.cloned.1.call-done = bf16[2560,1280]{1,0:T(8,128)(2,1)} async-done(((bf16[320,1280]{1,0:T(8,128)(2,1)}), bf16[2560,1280]{1,0:T(8,128)(2,1)}) %all-gather.8.cloned.1.call-update) | async-done | bytes 6553616 | tf_op jit(solution)/shard_map/all_gather | solution.py:112
  339.3 4.7 %fusion.5 = bf16[128,1280]{1,0:T(8,128)(2,1)} fusion(f32[128,1280]{1,0:T(8,128)S(1)} %fusion.22, bf16[128,2560]{0,1:T(8,128)(2,1)S(1)} %all_gather.14, bf16[2560,1280]{1,0:T(8,128)(2,1)} %all-gather.8.cloned.1.call-done), kind=kOutput, calls=%fused_computation.10 | convolution fusion | flops 839188480 | bytes 8192000 | tf_op jit(solution)/shard_map/dot_general | solution.py:71
  (8 shorter events, 0.1 us)
Async XLA Ops:
  6.5 47.8 %copy-start = (f32[16,5120]{1,0:T(8,128)S(1)}, f32[16,5120]{1,0:T(8,128)}, u32[]{:S(2)}) copy-start(f32[16,5120]{1,0:T(8,128)} %param.14) | copy-start | bytes 983044
  6.5 2.2 copy-start.7
  6.5 3.1 copy-start.4
  6.5 3.1 copy-start.3
  6.5 44.2 %all-gather.4.cloned.1.call-start = ((), (), s32[]{:S(2)}) async-start(), calls=%async_computation | async-start | bytes 1638400 | tf_op jit(solution)/shard_map/all_gather | solution.py:87
  7.3 243.5 %all-gather.6.cloned.1.call-start = ((), (), s32[]{:S(2)}) async-start(), calls=%async_computation.1 | async-start | bytes 22118400 | tf_op jit(solution)/shard_map/all_gather | solution.py:100
  8.0 331.3 %all-gather.8.cloned.1.call-start = ((), (), s32[]{:S(2)}) async-start(), calls=%async_computation.2 | async-start | bytes 7372800 | tf_op jit(solution)/shard_map/all_gather | solution.py:112
  50.8 3.6 %copy-start.1 = (bf16[128,5120]{1,0:T(8,128)(2,1)S(1)}, bf16[128,5120]{1,0:T(8,128)(2,1)}, u32[]{:S(2)}) copy-start(bf16[128,5120]{1,0:T(8,128)(2,1)} %all-gather.4.cloned.1.call-done) | copy-start | bytes 3932164
  52.5 3.4 copy-start.2
  262.5 0.8 copy-start.5
  262.6 0.8 copy-start.6
Sparse Core Ops, SparseCore 0:
  9.2 41.5 all-gather.3
  52.6 198.2 all-gather.5
  252.6 86.6 all-gather.7
where the time goes:
time: 352 us; the launch traced here: 350 us
  waiting for transfers between devices  288 us (82%)
  blocking collectives  23.1 us (7%)
  matrix products  20.2 us (6%)
  between operations  13.3 us (4%)
  other arithmetic  5.19 us (1%)
    all_gather x1, waiting for transfers between devices, shards(): lax.all_gather(w_qkv, 'row', axis=0, tiled=True)  194 us
    all_gather x1, waiting for transfers between devices, shards(): lax.all_gather(w_out, 'row', axis=0, tiled=True)  51.7 us
    all_gather x1, waiting for transfers between devices, shards(): features = lax.all_gather(tokens, 'col', axis=1, tiled=True)  40.7 us
    all_gather x1, blocking collectives, shards(): all_heads = lax.all_gather(attended, 'col', axis=1, tiled=True)  23.1 us
    dot_general x2, matrix products, add_panel(): return jnp.dot(left_side, panel, preferred_element_type=jnp.float32)  16.4 us
  transfers between devices with their start and end apart: 3, of which 3 were waited for; matrix products, arithmetic and copies ran while one was open for 6% of the time, Pallas kernels for 0%

commit v1 on v0

v1 whole, which is shorter than its diff:
```python
import math

import jax
import jax.numpy as jnp
from jax import lax
from jax.experimental import pallas as pl
from jax.experimental.pallas import tpu as pltpu
from jax.sharding import PartitionSpec as P

HD = 128
EPS = 1e-06
MESH = pl.DeviceIdType.MESH


def clip_places(first_row, row_count, clip_lengths):
    clip_ends = jnp.cumsum(clip_lengths, dtype=jnp.int32)
    token_index = first_row + jnp.arange(row_count, dtype=jnp.int32)
    passed = clip_ends[None, :] <= token_index[:, None]
    clip_number = jnp.sum(passed.astype(jnp.int32), axis=1, dtype=jnp.int32)
    clip_start = jnp.sum(jnp.where(passed, clip_lengths[None, :], 0), axis=1, dtype=jnp.int32)
    return (clip_number, token_index - clip_start)


def remote(src, dst, send, recv, device):
    return pltpu.make_async_remote_copy(
        src_ref=src, dst_ref=dst, send_sem=send, recv_sem=recv, device_id=device, device_id_type=MESH
    )


class Place:
    def __init__(self):
        row = lax.axis_index("row")
        depth = lax.axis_index("depth")
        self.zh = lax.axis_index("col")
        self.zl = row // 4
        self.x = row % 4
        self.y = depth // 2
        self.core = depth % 2
        self.z = self.zh * 2 + self.zl

    def at(self, x=None, y=None, z=None, core=None):
        x = self.x if x is None else x % 4
        y = self.y if y is None else y % 4
        z = self.z if z is None else z % 8
        core = self.core if core is None else core
        return ((z % 2) * 4 + x, z // 2, y * 2 + core)


class Weights:
    def __init__(self, at, tile, buf, sems, by_columns):
        self.at, self.tile, self.buf, self.by_columns = at, tile, buf, by_columns
        self.rows, self.cols = tile.shape
        (self.sx, self.rx, self.sf, self.rf, self.sy, self.ry, self.sc, self.rc, self.own) = sems

    def cut(self, ref, first, quarter, core):
        quarter_rows = self.rows // 4
        if self.by_columns:
            half = self.cols // 2
            return ref.at[
                pl.ds(pl.multiple_of(first + quarter * quarter_rows, 16), quarter_rows),
                pl.ds(pl.multiple_of(core * half, 128), half),
            ]
        half = quarter_rows // 2
        return ref.at[pl.ds(pl.multiple_of(first + quarter * quarter_rows + core * half, 16), half), :]

    def slot(self, x, quarter, core=None):
        core = self.at.core if core is None else core
        return self.cut(self.buf, (x % 4) * self.rows, quarter % 4, core)

    def x1(self, side, i):
        a = self.at
        to = a.x + 1 if side == 0 else a.x - 1
        return remote(
            self.cut(self.tile, 0, (a.y + i) % 4, a.core),
            self.slot(a.x, a.y + i),
            self.sx.at[side, i],
            self.rx.at[side, i],
            a.at(x=to),
        )

    def x2(self, side):
        a = self.at
        frm = a.x - 1 if side == 0 else a.x + 1
        to = a.x + 1 if side == 0 else a.x - 1
        ref = self.slot(frm, a.y + side)
        return remote(ref, ref, self.sf.at[side], self.rf.at[side], a.at(x=to))

    def y1(self, t, side):
        a = self.at
        ref = self.slot(a.x + t, a.y + side)
        to = a.y + 1 if side == 0 else a.y - 1
        return remote(ref, ref, self.sy.at[t - 1, side], self.ry.at[t - 1, side], a.at(y=to))

    def c1(self, t, i):
        a = self.at
        ref = self.slot(a.x + t, a.y + i)
        return remote(ref, ref, self.sc.at[t - 1, i], self.rc.at[t - 1, i], a.at(core=1 - a.core))

    def local(self):
        first = pl.multiple_of(self.at.x * self.rows, 16)
        return pltpu.make_async_copy(self.tile, self.buf.at[pl.ds(first, self.rows), :], self.own)

    def start(self):
        for side, i in ((0, 0), (1, 1), (0, 1), (1, 0)):
            self.x1(side, i).start()
        self.local().start()

    def near(self):
        for side in (0, 1):
            t = 3 if side == 0 else 1
            self.x1(side, side).wait_recv()
            self.x2(side).start()
            self.y1(t, side).start()
            self.c1(t, side).start()
        for side in (0, 1):
            t = 3 if side == 0 else 1
            self.x1(side, 1 - side).wait_recv()
            self.y1(t, 1 - side).start()
            self.c1(t, 1 - side).start()

    def far(self):
        for side in (0, 1):
            self.x2(side).wait_recv()
            self.y1(2, side).start()
            self.c1(2, side).start()

    def across(self):
        for t in (3, 1, 2):
            for side in (0, 1):
                self.y1(t, side).wait_recv()
                self.c1(t, 3 if side == 0 else 2).start()

    def ready(self):
        self.local().wait()
        for t in (3, 1, 2):
            for i in range(4):
                self.c1(t, i).wait_recv()

    def drain(self):
        for side in (0, 1):
            for i in (0, 1):
                self.x1(side, i).wait_send()
            self.x2(side).wait_send()
        for t in (1, 2, 3):
            for side in (0, 1):
                self.y1(t, side).wait_send()
            for i in range(4):
                self.c1(t, i).wait_send()


class Spread:
    def __init__(self, at, src, buf, sems):
        self.at, self.src, self.buf = at, src, buf
        self.width = src.shape[1]
        self.send, self.recv, self.relay_send = sems

    def view(self, slot, half):
        column = pl.multiple_of((slot // 2) * self.width, 128)
        return self.buf.at[slot % 2, pl.ds(half * 64, 64), pl.ds(column, self.width)]

    def out(self, o, half):
        a = self.at
        slot = a.z % 4
        to = 2 * ((a.z // 2 + o) % 4) + a.z // 4
        return remote(
            self.src.at[pl.ds(half * 64, 64), :],
            self.view(slot, half),
            self.send.at[o, half],
            self.recv.at[slot, half],
            a.at(z=to),
        )

    def keep(self, half):
        slot = self.at.z % 4
        return pltpu.make_async_copy(
            self.src.at[pl.ds(half * 64, 64), :], self.view(slot, half), self.recv.at[slot, half]
        )

    def came(self, slot, half):
        ref = self.view(slot, half)
        pltpu.make_async_copy(ref, ref, self.recv.at[slot, half]).wait()

    def forward(self, m, half):
        a = self.at
        slot = a.z % 2 + 2 * m
        ref = self.view(slot, half)
        to = a.z + 2 if half == 0 else a.z - 2
        return remote(ref, ref, self.relay_send.at[m], self.recv.at[slot, half], a.at(z=to))

    def on_ring(self):
        return self.at.z % 2 == self.at.z // 4

    def relation(self, m):
        a = self.at
        return (a.z // 2 - (2 * (a.z % 2) + m) + 4) % 4

    def start(self):
        for o in (1, 3):
            for half in (0, 1):
                self.out(o, half).start()

        @pl.when(self.on_ring())
        def _():
            for half in (0, 1):
                self.keep(half).start()

        @pl.when(jnp.logical_not(self.on_ring()))
        def _():
            for o in (0, 2):
                for half in (0, 1):
                    self.out(o, half).start()

    def relay(self):
        for m in (0, 1):
            rel = self.relation(m)
            slot = self.at.z % 2 + 2 * m

            @pl.when(rel == 1)
            def _():
                self.came(slot, 0)
                self.forward(m, 0).start()

            @pl.when(rel == 3)
            def _():
                self.came(slot, 1)
                self.forward(m, 1).start()

    def ready(self):
        for m in (0, 1):
            rel = self.relation(m)
            slot = self.at.z % 2 + 2 * m

            @pl.when(rel != 1)
            def _():
                self.came(slot, 0)

            @pl.when(rel != 3)
            def _():
                self.came(slot, 1)

            other = 1 - self.at.z % 2 + 2 * m
            self.came(other, 0)
            self.came(other, 1)

    def drain(self):
        for o in (1, 3):
            for half in (0, 1):
                self.out(o, half).wait_send()

        @pl.when(jnp.logical_not(self.on_ring()))
        def _():
            for o in (0, 2):
                for half in (0, 1):
                    self.out(o, half).wait_send()

        for m in (0, 1):
            rel = self.relation(m)

            @pl.when(rel == 1)
            def _():
                self.forward(m, 0).wait_send()

            @pl.when(rel == 3)
            def _():
                self.forward(m, 1).wait_send()


def block_kernel(
    tokens, ids, shift, scale, gate, wq, wo, qg, kg, cosine, sine, mask, out,
    wq_all, wo_all, mod, a1, att, a2, row_a, row_b, stat_in, stat_col, stats,
    home1, mine1, theirs1, home2, mine2, theirs2, acc1, acc2,
    stat_send, stat_recv, c1_send, c1_recv, c2_send, c2_recv,
    qs0, qs1, qs2, qs3, qs4, qs5, qs6, qs7, qs8,
    os0, os1, os2, os3, os4, os5, os6, os7, os8,
    as0, as1, as2, bs0, bs1, bs2,
):
    at = Place()
    wide = tokens.shape[1]
    heads = qg.shape[0]
    buckets = shift.shape[0]

    barrier = pltpu.get_barrier_semaphore()
    friends = [at.at(z=at.z + o) for o in range(1, 8)]
    friends += [at.at(x=at.x + 1), at.at(x=at.x + 3), at.at(y=at.y + 1), at.at(y=at.y + 3)]
    friends += [at.at(core=1 - at.core)]
    for friend in friends:
        pl.semaphore_signal(barrier, inc=1, device_id=friend, device_id_type=MESH)
    pl.semaphore_wait(barrier, len(friends))

    qkv = Weights(at, wq, wq_all, (qs0, qs1, qs2, qs3, qs4, qs5, qs6, qs7, qs8), False)
    proj = Weights(at, wo, wo_all, (os0, os1, os2, os3, os4, os5, os6, os7, os8), True)
    one = Spread(at, mod, a1, (as0, as1, as2))
    two = Spread(at, att, a2, (bs0, bs1, bs2))

    qkv.start()

    lane = lax.broadcasted_iota(jnp.int32, (16, HD), 1)

    @pl.loop(0, 8)
    def _(i):
        rows = pl.ds(pl.multiple_of(i * 16, 16), 16)
        part = tokens[rows, :].astype(jnp.float32)
        mean = jnp.sum(part, axis=1, keepdims=True) * (1.0 / wide)
        part = part - mean
        spread = jnp.sum(part * part, axis=1, keepdims=True)
        stat_in[rows, :] = jnp.where(lane == 0, mean, jnp.where(lane == 1, spread, 0.0))

    stats[at.zh] = stat_in[...].T[0:8, :]

    def stat_copy(o):
        ref = stats.at[at.zh]
        return remote(ref, ref, stat_send.at[o - 1], stat_recv.at[o - 1], at.at(z=at.z + 2 * o))

    for o in (1, 3, 2):
        stat_copy(o).start()

    one_hot = (ids[...] == lax.broadcasted_iota(jnp.int32, (HD, buckets), 1)).astype(jnp.float32)
    here = pl.ds(pl.multiple_of(at.zh * wide, 128), wide)
    row_a[...] = 1.0 + jnp.dot(
        one_hot, scale[:, here], precision=lax.Precision.HIGHEST, preferred_element_type=jnp.float32
    )
    row_b[...] = jnp.dot(
        one_hot, shift[:, here], precision=lax.Precision.HIGHEST, preferred_element_type=jnp.float32
    )

    for o in (1, 3, 2):
        stat_copy(o).wait_recv()
    means = [stats[c][0:1, :] for c in range(4)]
    mean = (means[0] + means[1] + means[2] + means[3]) * 0.25
    total = jnp.zeros_like(mean)
    for c in range(4):
        apart = means[c] - mean
        total = total + stats[c][1:2, :] + wide * (apart * apart)
    rstd = lax.rsqrt(total * (1.0 / (4 * wide)) + EPS)
    index = lax.broadcasted_iota(jnp.int32, (HD, HD), 0)
    stat_col[...] = jnp.where(index == 0, mean, jnp.where(index == 1, rstd, 0.0)).T

    @pl.loop(0, 8)
    def _(i):
        rows = pl.ds(pl.multiple_of(i * 16, 16), 16)
        normed = (tokens[rows, :].astype(jnp.float32) - stat_col[rows, 0:1]) * stat_col[rows, 1:2]
        mod[rows, :] = (normed * row_a[rows, :] + row_b[rows, :]).astype(jnp.bfloat16)

    one.start()
    qkv.near()
    proj.start()
    qkv.far()
    one.relay()
    qkv.across()
    proj.near()
    proj.far()
    row_a[...] = jnp.dot(
        one_hot, gate[...], precision=lax.Precision.HIGHEST, preferred_element_type=jnp.float32
    )
    qkv.ready()
    one.ready()

    partner = at.at(z=at.zh * 2 + 1 - at.zl)
    own_rows = pl.ds(pl.multiple_of(at.zl * HD, HD), HD)
    other_rows = pl.ds(pl.multiple_of((1 - at.zl) * HD, HD), HD)

    def swap1(h):
        return remote(mine1.at[h], theirs1.at[h], c1_send.at[h], c1_recv.at[h], partner)

    def swap2(h):
        return remote(mine2.at[h], theirs2.at[h], c2_send.at[h], c2_recv.at[h], partner)

    @pl.loop(0, heads)
    def _(h):
        columns = pl.ds(pl.multiple_of(h * (3 * HD), HD), 3 * HD)
        left = a1[...].reshape(2 * HD, a1.shape[2])
        acc1[...] = jnp.dot(left, wq_all[:, columns], preferred_element_type=jnp.float32)
        mine1[h] = acc1[other_rows, :].astype(jnp.bfloat16)
        swap1(h).start()
        home1[h] = acc1[own_rows, :]

    proj.across()

    def rotate(vectors, gains):
        power = jnp.mean(vectors * vectors, axis=-1, keepdims=True)
        vectors = vectors * lax.rsqrt(power + EPS) * gains
        turned = pltpu.roll(vectors, HD // 2, axis=1)
        return (vectors * cosine[...] + turned * sine[...]).astype(jnp.bfloat16)

    @pl.loop(0, heads)
    def _(h):
        swap1(h).wait_recv()
        joined = home1[h] + theirs1[h].astype(jnp.float32)
        query = rotate(joined[:, 0:HD], qg[pl.ds(h, 1), :])
        key = rotate(joined[:, HD : 2 * HD], kg[pl.ds(h, 1), :])
        value = joined[:, 2 * HD : 3 * HD].astype(jnp.bfloat16)
        scores = lax.dot_general(
            query, key, (((1,), (1,)), ((), ())), preferred_element_type=jnp.float32
        ) * (1.0 / math.sqrt(HD))
        raised = jnp.where(mask[...] > 0.0, jnp.exp(scores), 0.0)
        weights = (raised / jnp.sum(raised, axis=-1, keepdims=True)).astype(jnp.bfloat16)
        columns = pl.ds(pl.multiple_of(h * HD, HD), HD)
        att[:, columns] = jnp.dot(weights, value, preferred_element_type=jnp.float32).astype(
            jnp.bfloat16
        )

    two.start()
    proj.ready()
    two.relay()
    two.ready()

    pieces, piece = home2.shape[0], home2.shape[2]

    @pl.loop(0, pieces)
    def _(n):
        columns = pl.ds(pl.multiple_of(n * piece, HD), piece)
        left = a2[...].reshape(2 * HD, a2.shape[2])
        acc2[...] = jnp.dot(left, wo_all[:, columns], preferred_element_type=jnp.float32)
        mine2[n] = acc2[other_rows, :].astype(jnp.bfloat16)
        swap2(n).start()
        home2[n] = acc2[own_rows, :]

    qkv.drain()
    proj.drain()
    one.drain()
    two.drain()
    for o in (1, 2, 3):
        stat_copy(o).wait_send()

    @pl.loop(0, heads)
    def _(h):
        swap1(h).wait_send()

    @pl.loop(0, pieces)
    def _(n):
        columns = pl.ds(pl.multiple_of(n * piece, HD), piece)
        swap2(n).wait_recv()
        projected = home2[n] + theirs2[n].astype(jnp.float32)
        out[:, columns] = (row_a[:, columns] * projected).astype(jnp.bfloat16)

    @pl.loop(0, pieces)
    def _(n):
        swap2(n).wait_send()


def shards(
    tokens, bucket_ids, clip_lengths, shift_table, scale_table, gate_table, w_qkv, q_gain, k_gain, w_out
):
    rows, wide = tokens.shape
    heads = w_qkv.shape[1] // (3 * HD)
    first_row = lax.axis_index(("row", "depth")) * rows
    clip_number, position = clip_places(first_row, rows, clip_lengths)
    half = HD // 2
    inverse = 10000.0 ** (-jnp.arange(half, dtype=jnp.float32) / half)
    angles = position.astype(jnp.float32)[:, None] * inverse[None, :]
    cosine, sine = jnp.cos(angles), jnp.sin(angles)
    cosine = jnp.concatenate([cosine, cosine], axis=1)
    sine = jnp.concatenate([-sine, sine], axis=1)
    mask = (clip_number[:, None] == clip_number[None, :]).astype(jnp.float32)

    pieces = 5
    piece = wide // pieces
    bf16, f32 = jnp.bfloat16, jnp.float32
    dma = pltpu.SemaphoreType.DMA
    weight_sems = [dma((2, 2)), dma((2, 2)), dma((2,)), dma((2,)), dma((3, 2)), dma((3, 2)), dma((3, 4)), dma((3, 4)), dma]
    spread_sems = [dma((4, 2)), dma((4, 2)), dma((2,))]
    vmem = pl.BlockSpec(memory_space=pltpu.VMEM)
    hbm = pl.BlockSpec(memory_space=pl.ANY)
    return pl.pallas_call(
        block_kernel,
        out_shape=jax.ShapeDtypeStruct((rows, wide), bf16),
        in_specs=[vmem] * 5 + [hbm] * 2 + [vmem] * 5,
        out_specs=vmem,
        scratch_shapes=[
            pltpu.VMEM((4 * w_qkv.shape[0], w_qkv.shape[1]), bf16),
            pltpu.VMEM((4 * w_out.shape[0], w_out.shape[1]), bf16),
            pltpu.VMEM((rows, wide), bf16),
            pltpu.VMEM((2, rows, 2 * wide), bf16),
            pltpu.VMEM((rows, heads * HD), bf16),
            pltpu.VMEM((2, rows, 2 * heads * HD), bf16),
            pltpu.VMEM((rows, wide), f32),
            pltpu.VMEM((rows, wide), f32),
            pltpu.VMEM((rows, HD), f32),
            pltpu.VMEM((rows, HD), f32),
            pltpu.VMEM((4, 8, rows), f32),
            pltpu.VMEM((heads, rows, 3 * HD), f32),
            pltpu.VMEM((heads, rows, 3 * HD), bf16),
            pltpu.VMEM((heads, rows, 3 * HD), bf16),
            pltpu.VMEM((pieces, rows, piece), f32),
            pltpu.VMEM((pieces, rows, piece), bf16),
            pltpu.VMEM((pieces, rows, piece), bf16),
            pltpu.VMEM((2 * rows, 3 * HD), f32),
            pltpu.VMEM((2 * rows, piece), f32),
            dma((3,)), dma((3,)),
            dma((heads,)), dma((heads,)),
            dma((pieces,)), dma((pieces,)),
        ]
        + weight_sems + weight_sems + spread_sems + spread_sems,
        compiler_params=pltpu.CompilerParams(
            collective_id=0, has_side_effects=True, vmem_limit_bytes=52 * 1024 * 1024
        ),
    )(
        tokens, bucket_ids.reshape(rows, 1), shift_table, scale_table, gate_table, w_qkv, w_out,
        q_gain.reshape(heads, HD), k_gain.reshape(heads, HD), cosine, sine, mask,
    )


def solution(mesh):
    in_specs = (
        P(("row", "depth"), "col"),
        P(("row", "depth")),
        P(),
        P(),
        P(),
        P(None, "col"),
        P("row", "col"),
        P("col"),
        P("col"),
        P("row", "col"),
    )
    out_specs = P(("row", "depth"), "col")
    return jax.shard_map(shards, mesh=mesh, in_specs=in_specs, out_specs=out_specs, check_vma=False)
```

time: 352 us -> 99.7 us (0.28)
  the two profiles are of different devices: /device:TPU:24 before, /device:TPU:80 now
where the time goes in v1:
time: 99.7 us; the launch traced here: 99.4 us
  Pallas kernels  90.4 us (91%)
  local copies, waits for them, and re-layouts  7.41 us (7%)
  other arithmetic  1.47 us (1%)
    pallas_call x1, Pallas kernels, shards(): pl.pallas_call(block_kernel, out_shape=jax.ShapeDtypeStruct((rows, wide),...  90.4 us
    unnamed x13, local copies, waits for them, and re-layouts  5.9 us

profile of v1, /device:TPU:80, one launch (start us, length us, event | category | flops | bytes accessed | tf_op | source)
XLA Modules:
  0.0 99.4 jit_solution(13181756872064130129)
XLA Ops:
  0.0 0.7 copy.15
  0.8 0.1 reduce-window.8
  0.9 0.1 reduce
  1.0 0.8 fusion.1
  1.7 0.1 compare_convert_fusion.mask
  1.8 0.8 copy.16.ids
  2.6 0.3 fusion.2
  2.9 0.1 pad_maximum_fusion
  3.0 0.0 copy-start
  3.0 1.0 copy-done
  4.0 0.0 copy-start.1
  4.0 1.0 copy-done.1
  5.0 0.0 copy-start.2
  5.0 1.0 copy-done.2
  5.9 0.0 copy-start.3
  5.9 0.9 copy-done.3
  6.8 0.0 copy-start.4
  6.8 0.7 copy-done.4
  7.5 0.0 copy-start.5
  7.5 0.7 copy-done.5
  8.2 90.4 %shard_map.100 = bf16[128,1280]{1,0:T(8,128)(2,1)S(1)} custom-call(bf16[128,1280]{1,0:T(8,128)(2,1)S(1)} %copy-done, s32[128,1]{1,0:T(8,128)S(1)} %copy.16.ids, f32[16,5120]{1,0:T(8,128)S(1)} %copy-done.1, f32[16,5120]{1,0:T(8,128)S(1)} %copy-done.2, f32[16,1280]{1,0:T(8,128)S(1)} %copy-done.3, bf16[640,1920]{1,0:T(8,128)(2,1)} %wq.1, bf16[320,1280]{1,0:T(8,128)(2,1)} %wo.1, ...), custom_call_target="tpu_custom_call" | custom-call | tf_op jit(solution)/shard_map/pallas_call | solution.py:464
  98.7 0.7 copy.18
  (3 shorter events, 0.0 us)
Async XLA Ops:
  3.0 1.0 copy-start
  4.0 1.0 copy-start.1
  5.0 1.0 copy-start.2
  5.9 0.9 copy-start.3
  6.8 0.7 copy-start.4
  7.5 0.7 copy-start.5

commit v2 on v1

--- a/solution.py
+++ b/solution.py
@@ -1,3 +1,4 @@
+import functools
 import math
 
 import jax
@@ -10,15 +11,6 @@
 HD = 128
 EPS = 1e-06
 MESH = pl.DeviceIdType.MESH
-
-
-def clip_places(first_row, row_count, clip_lengths):
-    clip_ends = jnp.cumsum(clip_lengths, dtype=jnp.int32)
-    token_index = first_row + jnp.arange(row_count, dtype=jnp.int32)
-    passed = clip_ends[None, :] <= token_index[:, None]
-    clip_number = jnp.sum(passed.astype(jnp.int32), axis=1, dtype=jnp.int32)
-    clip_start = jnp.sum(jnp.where(passed, clip_lengths[None, :], 0), axis=1, dtype=jnp.int32)
-    return (clip_number, token_index - clip_start)
 
 
 def remote(src, dst, send, recv, device):
@@ -149,135 +141,139 @@
 
 
 class Spread:
+    SENDS = (
+        ((2, 0), (6, 1), (2, 1), (6, 0)),
+        ((1, 1), (7, 1), (3, 0), (5, 0), (1, 0), (7, 0)),
+        ((2, 0), (6, 1), (2, 1), (6, 0)),
+        ((1, 0), (1, 1), (5, 0), (5, 1), (7, 0), (7, 1)),
+        ((7, 1), (3, 0), (3, 1), (5, 0), (1, 0), (1, 1), (7, 0)),
+        ((2, 0), (6, 1), (2, 1), (6, 0)),
+        ((1, 1), (5, 0), (5, 1), (3, 0), (1, 0), (7, 0), (7, 1)),
+        ((2, 0), (2, 1), (6, 0), (6, 1)),
+    )
+    RELAYS = (
+        ((1, 1, 6), (2, 1, 6)),
+        ((3, 0, 2), (3, 1, 2)),
+        ((0, 0, 2), (1, 1, 2)),
+        ((0, 1, 6), (1, 1, 6)),
+        ((3, 0, 2), (2, 0, 2), (3, 1, 2)),
+        (),
+        ((0, 1, 6),),
+        ((1, 0, 2), (2, 1, 2)),
+    )
+
     def __init__(self, at, src, buf, sems):
         self.at, self.src, self.buf = at, src, buf
-        self.width = src.shape[1]
-        self.send, self.recv, self.relay_send = sems
+        self.half, self.width = src.shape[0] // 2, src.shape[1]
+        self.send, self.recv = sems
 
     def view(self, slot, half):
-        column = pl.multiple_of((slot // 2) * self.width, 128)
-        return self.buf.at[slot % 2, pl.ds(half * 64, 64), pl.ds(column, self.width)]
-
-    def out(self, o, half):
-        a = self.at
-        slot = a.z % 4
-        to = 2 * ((a.z // 2 + o) % 4) + a.z // 4
+        column = slot // 2 * self.width
+        return self.buf.at[slot % 2, pl.ds(half * self.half, self.half), pl.ds(column, self.width)]
+
+    def own(self, half):
+        return self.src.at[pl.ds(half * self.half, self.half), :]
+
+    def out(self, z, i):
+        go, half = self.SENDS[z][i]
+        slot = z % 4
         return remote(
-            self.src.at[pl.ds(half * 64, 64), :],
-            self.view(slot, half),
-            self.send.at[o, half],
-            self.recv.at[slot, half],
-            a.at(z=to),
+            self.own(half), self.view(slot, half), self.send.at[i], self.recv.at[slot, half], self.at.at(z=z + go)
         )
 
-    def keep(self, half):
-        slot = self.at.z % 4
-        return pltpu.make_async_copy(
-            self.src.at[pl.ds(half * 64, 64), :], self.view(slot, half), self.recv.at[slot, half]
-        )
+    def keep(self, z, half):
+        slot = z % 4
+        return pltpu.make_async_copy(self.own(half), self.view(slot, half), self.recv.at[slot, half])
 
     def came(self, slot, half):
         ref = self.view(slot, half)
         pltpu.make_async_copy(ref, ref, self.recv.at[slot, half]).wait()
 
-    def forward(self, m, half):
-        a = self.at
-        slot = a.z % 2 + 2 * m
+    def forward(self, z, i):
+        slot, half, go = self.RELAYS[z][i]
         ref = self.view(slot, half)
-        to = a.z + 2 if half == 0 else a.z - 2
-        return remote(ref, ref, self.relay_send.at[m], self.recv.at[slot, half], a.at(z=to))
-
-    def on_ring(self):
-        return self.at.z % 2 == self.at.z // 4
-
-    def relation(self, m):
-        a = self.at
-        return (a.z // 2 - (2 * (a.z % 2) + m) + 4) % 4
+        return remote(
+            ref, ref, self.send.at[len(self.SENDS[z]) + i], self.recv.at[slot, half], self.at.at(z=z + go)
+        )
+
+    def each(self, body):
+        for z in range(8):
+            pl.when(self.at.z == z)(functools.partial(body, z))
 
     def start(self):
-        for o in (1, 3):
-            for half in (0, 1):
-                self.out(o, half).start()
-
-        @pl.when(self.on_ring())
-        def _():
-            for half in (0, 1):
-                self.keep(half).start()
-
-        @pl.when(jnp.logical_not(self.on_ring()))
-        def _():
-            for o in (0, 2):
+        def body(z):
+            for i in range(len(self.SENDS[z])):
+                self.out(z, i).start()
+            if z % 2 == z // 4:
                 for half in (0, 1):
-                    self.out(o, half).start()
+                    self.keep(z, half).start()
+
+        self.each(body)
 
     def relay(self):
-        for m in (0, 1):
-            rel = self.relation(m)
-            slot = self.at.z % 2 + 2 * m
-
-            @pl.when(rel == 1)
-            def _():
-                self.came(slot, 0)
-                self.forward(m, 0).start()
-
-            @pl.when(rel == 3)
-            def _():
-                self.came(slot, 1)
-                self.forward(m, 1).start()
+        def body(z):
+            for i, (slot, half, _) in enumerate(self.RELAYS[z]):
+                self.came(slot, half)
+                self.forward(z, i).start()
+
+        self.each(body)
 
     def ready(self):
-        for m in (0, 1):
-            rel = self.relation(m)
-            slot = self.at.z % 2 + 2 * m
-
-            @pl.when(rel != 1)
-            def _():
-                self.came(slot, 0)
-
-            @pl.when(rel != 3)
-            def _():
-                self.came(slot, 1)
-
-            other = 1 - self.at.z % 2 + 2 * m
-            self.came(other, 0)
-            self.came(other, 1)
+        def body(z):
+            taken = [(slot, half) for slot, half, _ in self.RELAYS[z]]
+            for slot in range(4):
+                for half in (0, 1):
+                    if (slot, half) not in taken:
+                        self.came(slot, half)
+
+        self.each(body)
 
     def drain(self):
-        for o in (1, 3):
-            for half in (0, 1):
-                self.out(o, half).wait_send()
-
-        @pl.when(jnp.logical_not(self.on_ring()))
-        def _():
-            for o in (0, 2):
-                for half in (0, 1):
-                    self.out(o, half).wait_send()
-
-        for m in (0, 1):
-            rel = self.relation(m)
-
-            @pl.when(rel == 1)
-            def _():
-                self.forward(m, 0).wait_send()
-
-            @pl.when(rel == 3)
-            def _():
-                self.forward(m, 1).wait_send()
+        def body(z):
+            for i in range(len(self.SENDS[z])):
+                self.out(z, i).wait_send()
+            for i in range(len(self.RELAYS[z])):
+                self.forward(z, i).wait_send()
+
+        self.each(body)
+
+
+def bucket_rows(pick, table):
+    first = table.astype(jnp.bfloat16)
+    rest = table - first.astype(jnp.float32)
+    second = rest.astype(jnp.bfloat16)
+    third = (rest - second.astype(jnp.float32)).astype(jnp.bfloat16)
+    terms = jnp.concatenate([first, second, third], axis=0)
+    return jnp.dot(pick, terms, preferred_element_type=jnp.float32)
 
 
 def block_kernel(
-    tokens, ids, shift, scale, gate, wq, wo, qg, kg, cosine, sine, mask, out,
+    tokens_in, ids_in, clips_in, shift_in, scale_in, gate_in, wq, wo, qg_in, kg_in, out,
+    tokens, ids, clips, shift, scale, gate, qg, kg, cosine, sine, mask, result, in_sem, out_sem,
     wq_all, wo_all, mod, a1, att, a2, row_a, row_b, stat_in, stat_col, stats,
     home1, mine1, theirs1, home2, mine2, theirs2, acc1, acc2,
     stat_send, stat_recv, c1_send, c1_recv, c2_send, c2_recv,
     qs0, qs1, qs2, qs3, qs4, qs5, qs6, qs7, qs8,
     os0, os1, os2, os3, os4, os5, os6, os7, os8,
-    as0, as1, as2, bs0, bs1, bs2,
+    as0, as1, bs0, bs1,
 ):
     at = Place()
     wide = tokens.shape[1]
-    heads = qg.shape[0]
+    heads = qg.shape[0] // HD
     buckets = shift.shape[0]
+    here = pl.ds(pl.multiple_of(at.zh * wide, 128), wide)
+    loads = [
+        pltpu.make_async_copy(src, dst, in_sem.at[i])
+        for i, (src, dst) in enumerate(
+            [
+                (tokens_in, tokens), (ids_in, ids), (scale_in.at[:, here], scale),
+                (shift_in.at[:, here], shift), (gate_in, gate), (clips_in, clips),
+                (qg_in, qg), (kg_in, kg),
+            ]
+        )
+    ]
+    for load in loads:
+        load.start()
 
     barrier = pltpu.get_barrier_semaphore()
     friends = [at.at(z=at.z + o) for o in range(1, 8)]
@@ -289,10 +285,11 @@
 
     qkv = Weights(at, wq, wq_all, (qs0, qs1, qs2, qs3, qs4, qs5, qs6, qs7, qs8), False)
     proj = Weights(at, wo, wo_all, (os0, os1, os2, os3, os4, os5, os6, os7, os8), True)
-    one = Spread(at, mod, a1, (as0, as1, as2))
-    two = Spread(at, att, a2, (bs0, bs1, bs2))
+    one = Spread(at, mod, a1, (as0, as1))
+    two = Spread(at, att, a2, (bs0, bs1))
 
     qkv.start()
+    loads[0].wait()
 
     lane = lax.broadcasted_iota(jnp.int32, (16, HD), 1)
 
@@ -314,14 +311,14 @@
     for o in (1, 3, 2):
         stat_copy(o).start()
 
-    one_hot = (ids[...] == lax.broadcasted_iota(jnp.int32, (HD, buckets), 1)).astype(jnp.float32)
-    here = pl.ds(pl.multiple_of(at.zh * wide, 128), wide)
-    row_a[...] = 1.0 + jnp.dot(
-        one_hot, scale[:, here], precision=lax.Precision.HIGHEST, preferred_element_type=jnp.float32
-    )
-    row_b[...] = jnp.dot(
-        one_hot, shift[:, here], precision=lax.Precision.HIGHEST, preferred_element_type=jnp.float32
-    )
+    for load in loads[1:]:
+        load.wait()
+    lanes = lax.broadcasted_iota(jnp.int32, (HD, HD), 1)
+    index = lax.broadcasted_iota(jnp.int32, (HD, HD), 0)
+    bucket = jnp.broadcast_to(ids[...].astype(jnp.float32), (HD, HD)).T.astype(jnp.int32)
+    pick = (bucket[:, 0 : 3 * buckets] == lanes[:, 0 : 3 * buckets] % buckets).astype(jnp.bfloat16)
+    row_a[...] = 1.0 + bucket_rows(pick, scale[...])
+    row_b[...] = bucket_rows(pick, shift[...])
 
     for o in (1, 3, 2):
         stat_copy(o).wait_recv()
@@ -332,7 +329,6 @@
         apart = means[c] - mean
         total = total + stats[c][1:2, :] + wide * (apart * apart)
     rstd = lax.rsqrt(total * (1.0 / (4 * wide)) + EPS)
-    index = lax.broadcasted_iota(jnp.int32, (HD, HD), 0)
     stat_col[...] = jnp.where(index == 0, mean, jnp.where(index == 1, rstd, 0.0)).T
 
     @pl.loop(0, 8)
@@ -342,6 +338,30 @@
         mod[rows, :] = (normed * row_a[rows, :] + row_b[rows, :]).astype(jnp.bfloat16)
 
     one.start()
+
+    count = clips.shape[1]
+    lengths = jnp.broadcast_to(clips[...], (8, count)).astype(jnp.bfloat16)
+    before = (
+        lax.broadcasted_iota(jnp.int32, (count, count), 0)
+        <= lax.broadcasted_iota(jnp.int32, (count, count), 1)
+    ).astype(jnp.bfloat16)
+    ends = jnp.dot(lengths, before, preferred_element_type=jnp.float32)[0:1, :]
+    first = (at.zl * 4 + at.x) * 8 + at.y * 2 + at.core
+    token = (first * HD + lax.broadcasted_iota(jnp.int32, (HD, count), 0)).astype(jnp.float32)
+    passed = ends <= token
+    clip = jnp.sum(jnp.where(passed, 1.0, 0.0), axis=1, keepdims=True)
+    begin = jnp.sum(
+        jnp.where(passed, clips[...].astype(jnp.float32), 0.0), axis=1, keepdims=True
+    )
+    clip = jnp.broadcast_to(clip, (HD, HD))
+    mask[...] = jnp.where(clip == clip.T, 1.0, 0.0)
+    half = HD // 2
+    power = (lanes[:, 0:half]).astype(jnp.float32) * (-math.log(10000.0) / half)
+    angles = (token[:, 0:1] - begin) * jnp.exp(power)
+    cosine_half, sine_half = jnp.cos(angles), jnp.sin(angles)
+    cosine[...] = jnp.concatenate([cosine_half, cosine_half], axis=1)
+    sine[...] = jnp.concatenate([-sine_half, sine_half], axis=1)
+
     qkv.near()
     proj.start()
     qkv.far()
@@ -349,18 +369,21 @@
     qkv.across()
     proj.near()
     proj.far()
-    row_a[...] = jnp.dot(
-        one_hot, gate[...], precision=lax.Precision.HIGHEST, preferred_element_type=jnp.float32
-    )
+    row_a[...] = bucket_rows(pick, gate[...])
     qkv.ready()
     one.ready()
 
+    pieces, piece = home2.shape[0], home2.shape[2]
     partner = at.at(z=at.zh * 2 + 1 - at.zl)
     own_rows = pl.ds(pl.multiple_of(at.zl * HD, HD), HD)
     other_rows = pl.ds(pl.multiple_of((1 - at.zl) * HD, HD), HD)
 
     def swap1(h):
         return remote(mine1.at[h], theirs1.at[h], c1_send.at[h], c1_recv.at[h], partner)
+
+    def store(n):
+        columns = pl.ds(pl.multiple_of(n * piece, HD), piece)
+        return pltpu.make_async_copy(result.at[n], out.at[:, columns], out_sem.at[n])
 
     def swap2(h):
         return remote(mine2.at[h], theirs2.at[h], c2_send.at[h], c2_recv.at[h], partner)
@@ -385,17 +408,17 @@
     @pl.loop(0, heads)
     def _(h):
         swap1(h).wait_recv()
+        head = pl.ds(pl.multiple_of(h * HD, HD), HD)
         joined = home1[h] + theirs1[h].astype(jnp.float32)
-        query = rotate(joined[:, 0:HD], qg[pl.ds(h, 1), :])
-        key = rotate(joined[:, HD : 2 * HD], kg[pl.ds(h, 1), :])
+        query = rotate(joined[:, 0:HD], qg[head].reshape(1, HD))
+        key = rotate(joined[:, HD : 2 * HD], kg[head].reshape(1, HD))
         value = joined[:, 2 * HD : 3 * HD].astype(jnp.bfloat16)
         scores = lax.dot_general(
             query, key, (((1,), (1,)), ((), ())), preferred_element_type=jnp.float32
         ) * (1.0 / math.sqrt(HD))
         raised = jnp.where(mask[...] > 0.0, jnp.exp(scores), 0.0)
         weights = (raised / jnp.sum(raised, axis=-1, keepdims=True)).astype(jnp.bfloat16)
-        columns = pl.ds(pl.multiple_of(h * HD, HD), HD)
-        att[:, columns] = jnp.dot(weights, value, preferred_element_type=jnp.float32).astype(
+        att[:, head] = jnp.dot(weights, value, preferred_element_type=jnp.float32).astype(
             jnp.bfloat16
         )
 
@@ -403,8 +426,6 @@
     proj.ready()
     two.relay()
     two.ready()
-
-    pieces, piece = home2.shape[0], home2.shape[2]
 
     @pl.loop(0, pieces)
     def _(n):
@@ -431,11 +452,13 @@
         columns = pl.ds(pl.multiple_of(n * piece, HD), piece)
         swap2(n).wait_recv()
         projected = home2[n] + theirs2[n].astype(jnp.float32)
-        out[:, columns] = (row_a[:, columns] * projected).astype(jnp.bfloat16)
+        result[n] = (row_a[:, columns] * projected).astype(jnp.bfloat16)
+        store(n).start()
 
     @pl.loop(0, pieces)
     def _(n):
         swap2(n).wait_send()
+        store(n).wait()
 
 
 def shards(
@@ -443,30 +466,33 @@
 ):
     rows, wide = tokens.shape
     heads = w_qkv.shape[1] // (3 * HD)
-    first_row = lax.axis_index(("row", "depth")) * rows
-    clip_number, position = clip_places(first_row, rows, clip_lengths)
-    half = HD // 2
-    inverse = 10000.0 ** (-jnp.arange(half, dtype=jnp.float32) / half)
-    angles = position.astype(jnp.float32)[:, None] * inverse[None, :]
-    cosine, sine = jnp.cos(angles), jnp.sin(angles)
-    cosine = jnp.concatenate([cosine, cosine], axis=1)
-    sine = jnp.concatenate([-sine, sine], axis=1)
-    mask = (clip_number[:, None] == clip_number[None, :]).astype(jnp.float32)
-
     pieces = 5
     piece = wide // pieces
     bf16, f32 = jnp.bfloat16, jnp.float32
     dma = pltpu.SemaphoreType.DMA
     weight_sems = [dma((2, 2)), dma((2, 2)), dma((2,)), dma((2,)), dma((3, 2)), dma((3, 2)), dma((3, 4)), dma((3, 4)), dma]
-    spread_sems = [dma((4, 2)), dma((4, 2)), dma((2,))]
-    vmem = pl.BlockSpec(memory_space=pltpu.VMEM)
-    hbm = pl.BlockSpec(memory_space=pl.ANY)
+    spread_sems = [dma((10,)), dma((4, 2))]
+    hbm = pl.BlockSpec(memory_space=pltpu.HBM)
     return pl.pallas_call(
         block_kernel,
         out_shape=jax.ShapeDtypeStruct((rows, wide), bf16),
-        in_specs=[vmem] * 5 + [hbm] * 2 + [vmem] * 5,
-        out_specs=vmem,
+        in_specs=[hbm] * 10,
+        out_specs=hbm,
         scratch_shapes=[
+            pltpu.VMEM((rows, wide), bf16),
+            pltpu.VMEM((1, rows), jnp.int32),
+            pltpu.VMEM((1, clip_lengths.shape[0]), jnp.int32),
+            pltpu.VMEM((shift_table.shape[0], wide), f32),
+            pltpu.VMEM((shift_table.shape[0], wide), f32),
+            pltpu.VMEM((shift_table.shape[0], wide), f32),
+            pltpu.VMEM((heads * HD,), f32),
+            pltpu.VMEM((heads * HD,), f32),
+            pltpu.VMEM((rows, HD), f32),
+            pltpu.VMEM((rows, HD), f32),
+            pltpu.VMEM((rows, rows), f32),
+            pltpu.VMEM((pieces, rows, piece), bf16),
+            dma((8,)),
+            dma((pieces,)),
             pltpu.VMEM((4 * w_qkv.shape[0], w_qkv.shape[1]), bf16),
             pltpu.VMEM((4 * w_out.shape[0], w_out.shape[1]), bf16),
             pltpu.VMEM((rows, wide), bf16),
@@ -492,11 +518,11 @@
         ]
         + weight_sems + weight_sems + spread_sems + spread_sems,
         compiler_params=pltpu.CompilerParams(
-            collective_id=0, has_side_effects=True, vmem_limit_bytes=52 * 1024 * 1024
+            collective_id=0, has_side_effects=True, vmem_limit_bytes=60 * 1024 * 1024
         ),
     )(
-        tokens, bucket_ids.reshape(rows, 1), shift_table, scale_table, gate_table, w_qkv, w_out,
-        q_gain.reshape(heads, HD), k_gain.reshape(heads, HD), cosine, sine, mask,
+        tokens, bucket_ids.reshape(1, rows), clip_lengths.reshape(1, -1), shift_table, scale_table, gate_table,
+        w_qkv, w_out, q_gain, k_gain,
     )
 
 

time: 99.7 us -> 92.6 us (0.929)
  the two profiles are of different devices: /device:TPU:80 before, /device:TPU:164 now
where the time goes in v2:
time: 92.6 us; the launch traced here: 92.5 us
  Pallas kernels  90.8 us (98%)
  local copies, waits for them, and re-layouts  1.72 us (2%)
    pallas_call x1, Pallas kernels, shards(): pl.pallas_call(block_kernel, out_shape=jax.ShapeDtypeStruct((rows, wide),...  90.8 us

profile of v2, /device:TPU:164, one launch (start us, length us, event | category | flops | bytes accessed | tf_op | source)
XLA Modules:
  0.0 92.5 jit_solution(1000480344509822697)
XLA Ops:
  0.0 90.8 %shard_map.100 = bf16[128,1280]{1,0:T(8,128)(2,1)} custom-call(bf16[128,1280]{1,0:T(8,128)(2,1)} %tokens_in.1, s32[1,128]{1,0:T(1,128)} %bitcast.2, s32[1,64]{1,0:T(1,128)} %bitcast.3, f32[16,5120]{1,0:T(8,128)} %shift_in.1, f32[16,5120]{1,0:T(8,128)} %scale_in.1, f32[16,1280]{1,0:T(8,128)} %gate_in.1, bf16[640,1920]{1,0:T(8,128)(2,1)} %wq.1, ...), custom_call_target="tpu_custom_call" | custom-call | tf_op jit(solution)/shard_map/pallas_call | solution.py:476
  90.8 1.7 %copy.12 = bf16[128,1280]{1,0:T(8,128)(2,1)} copy(bf16[128,1280]{1,0:T(8,128)(2,1)} %shard_map.100) | data formatting | bytes 655360

commit v3 on v2

--- a/solution.py
+++ b/solution.py
@@ -210,18 +210,19 @@
 
         self.each(body)
 
-    def relay(self):
+    def relay(self, turns=(0, 1, 2)):
         def body(z):
             for i, (slot, half, _) in enumerate(self.RELAYS[z]):
-                self.came(slot, half)
-                self.forward(z, i).start()
+                if i in turns:
+                    self.came(slot, half)
+                    self.forward(z, i).start()
 
         self.each(body)
 
-    def ready(self):
+    def ready(self, slots=(0, 1, 2, 3)):
         def body(z):
             taken = [(slot, half) for slot, half, _ in self.RELAYS[z]]
-            for slot in range(4):
+            for slot in slots:
                 for half in (0, 1):
                     if (slot, half) not in taken:
                         self.came(slot, half)
@@ -249,8 +250,8 @@
 
 def block_kernel(
     tokens_in, ids_in, clips_in, shift_in, scale_in, gate_in, wq, wo, qg_in, kg_in, out,
-    tokens, ids, clips, shift, scale, gate, qg, kg, cosine, sine, mask, result, in_sem, out_sem,
-    wq_all, wo_all, mod, a1, att, a2, row_a, row_b, stat_in, stat_col, stats,
+    tokens, ids, their_ids, clips, shift, scale, gate, qg, kg, cosine, sine, mask, result, in_sem, out_sem, id_sem,
+    wq_all, wo_all, raw, a1, att, a2, row_a, row_b, row_gate, stat_in, stat_col, stats,
     home1, mine1, theirs1, home2, mine2, theirs2, acc1, acc2,
     stat_send, stat_recv, c1_send, c1_recv, c2_send, c2_recv,
     qs0, qs1, qs2, qs3, qs4, qs5, qs6, qs7, qs8,
@@ -261,7 +262,7 @@
     wide = tokens.shape[1]
     heads = qg.shape[0] // HD
     buckets = shift.shape[0]
-    here = pl.ds(pl.multiple_of(at.zh * wide, 128), wide)
+    here = pl.ds(pl.multiple_of(at.zl * (2 * wide), 128), 2 * wide)
     loads = [
         pltpu.make_async_copy(src, dst, in_sem.at[i])
         for i, (src, dst) in enumerate(
@@ -285,11 +286,18 @@
 
     qkv = Weights(at, wq, wq_all, (qs0, qs1, qs2, qs3, qs4, qs5, qs6, qs7, qs8), False)
     proj = Weights(at, wo, wo_all, (os0, os1, os2, os3, os4, os5, os6, os7, os8), True)
-    one = Spread(at, mod, a1, (as0, as1))
+    one = Spread(at, tokens_in, raw, (as0, as1))
     two = Spread(at, att, a2, (bs0, bs1))
 
+    partner = at.at(z=at.zh * 2 + 1 - at.zl)
+    loads[1].wait()
+    id_copy = remote(ids, their_ids, id_sem.at[0], id_sem.at[1], partner)
+    id_copy.start()
+    one.start()
     qkv.start()
-    loads[0].wait()
+    for i, load in enumerate(loads):
+        if i != 1:
+            load.wait()
 
     lane = lax.broadcasted_iota(jnp.int32, (16, HD), 1)
 
@@ -302,43 +310,19 @@
         spread = jnp.sum(part * part, axis=1, keepdims=True)
         stat_in[rows, :] = jnp.where(lane == 0, mean, jnp.where(lane == 1, spread, 0.0))
 
-    stats[at.zh] = stat_in[...].T[0:8, :]
+    index = lax.broadcasted_iota(jnp.int32, (HD, HD), 0)
+    lanes = lax.broadcasted_iota(jnp.int32, (HD, HD), 1)
+    stats[at.z] = stat_in[...].T[0:8, :]
 
     def stat_copy(o):
-        ref = stats.at[at.zh]
-        return remote(ref, ref, stat_send.at[o - 1], stat_recv.at[o - 1], at.at(z=at.z + 2 * o))
-
-    for o in (1, 3, 2):
+        ref = stats.at[at.z]
+        return remote(ref, ref, stat_send.at[o - 1], stat_recv.at[o - 1], at.at(z=at.z + o))
+
+    for o in range(1, 8):
         stat_copy(o).start()
 
-    for load in loads[1:]:
-        load.wait()
-    lanes = lax.broadcasted_iota(jnp.int32, (HD, HD), 1)
-    index = lax.broadcasted_iota(jnp.int32, (HD, HD), 0)
-    bucket = jnp.broadcast_to(ids[...].astype(jnp.float32), (HD, HD)).T.astype(jnp.int32)
-    pick = (bucket[:, 0 : 3 * buckets] == lanes[:, 0 : 3 * buckets] % buckets).astype(jnp.bfloat16)
-    row_a[...] = 1.0 + bucket_rows(pick, scale[...])
-    row_b[...] = bucket_rows(pick, shift[...])
-
-    for o in (1, 3, 2):
-        stat_copy(o).wait_recv()
-    means = [stats[c][0:1, :] for c in range(4)]
-    mean = (means[0] + means[1] + means[2] + means[3]) * 0.25
-    total = jnp.zeros_like(mean)
-    for c in range(4):
-        apart = means[c] - mean
-        total = total + stats[c][1:2, :] + wide * (apart * apart)
-    rstd = lax.rsqrt(total * (1.0 / (4 * wide)) + EPS)
-    stat_col[...] = jnp.where(index == 0, mean, jnp.where(index == 1, rstd, 0.0)).T
-
-    @pl.loop(0, 8)
-    def _(i):
-        rows = pl.ds(pl.multiple_of(i * 16, 16), 16)
-        normed = (tokens[rows, :].astype(jnp.float32) - stat_col[rows, 0:1]) * stat_col[rows, 1:2]
-        mod[rows, :] = (normed * row_a[rows, :] + row_b[rows, :]).astype(jnp.bfloat16)
-
-    one.start()
-
+    qkv.near()
+    one.relay()
     count = clips.shape[1]
     lengths = jnp.broadcast_to(clips[...], (8, count)).astype(jnp.bfloat16)
     before = (
@@ -350,9 +334,7 @@
     token = (first * HD + lax.broadcasted_iota(jnp.int32, (HD, count), 0)).astype(jnp.float32)
     passed = ends <= token
     clip = jnp.sum(jnp.where(passed, 1.0, 0.0), axis=1, keepdims=True)
-    begin = jnp.sum(
-        jnp.where(passed, clips[...].astype(jnp.float32), 0.0), axis=1, keepdims=True
-    )
+    begin = jnp.sum(jnp.where(passed, clips[...].astype(jnp.float32), 0.0), axis=1, keepdims=True)
     clip = jnp.broadcast_to(clip, (HD, HD))
     mask[...] = jnp.where(clip == clip.T, 1.0, 0.0)
     half = HD // 2
@@ -362,19 +344,51 @@
     cosine[...] = jnp.concatenate([cosine_half, cosine_half], axis=1)
     sine[...] = jnp.concatenate([-sine_half, sine_half], axis=1)
 
-    qkv.near()
+    def bucket_rows_of(bucket, table):
+        bucket = jnp.broadcast_to(bucket[...].astype(jnp.float32), (HD, HD)).T.astype(jnp.int32)
+        pick = (bucket[:, 0 : 3 * buckets] == lanes[:, 0 : 3 * buckets] % buckets).astype(jnp.bfloat16)
+        return bucket_rows(pick, table[...])
+
+    row_a[at.zl] = 1.0 + bucket_rows_of(ids, scale)
+    row_b[at.zl] = bucket_rows_of(ids, shift)
+    row_gate[...] = bucket_rows_of(ids, gate)
+    id_copy.wait()
+    row_a[1 - at.zl] = 1.0 + bucket_rows_of(their_ids, scale)
+    row_b[1 - at.zl] = bucket_rows_of(their_ids, shift)
+
+    qkv.far()
     proj.start()
-    qkv.far()
-    one.relay()
     qkv.across()
-    proj.near()
-    proj.far()
-    row_a[...] = bucket_rows(pick, gate[...])
+
+    for o in range(1, 8):
+        stat_copy(o).wait_recv()
+
+    for block in (0, 1):
+        parts = [stats[2 * c + block] for c in range(4)]
+        mean = (parts[0][0:1] + parts[1][0:1] + parts[2][0:1] + parts[3][0:1]) * 0.25
+        total = jnp.zeros_like(mean)
+        for part in parts:
+            apart = part[0:1] - mean
+            total = total + part[1:2] + wide * (apart * apart)
+        rstd = lax.rsqrt(total * (1.0 / (4 * wide)) + EPS)
+        stat_col[block] = jnp.where(index == 0, mean, jnp.where(index == 1, rstd, 0.0)).T
+
+    for slot in range(4):
+        one.ready((slot,))
+        block, part = slot % 2, pl.ds(slot // 2 * wide, wide)
+
+        @pl.loop(0, 8)
+        def _(i):
+            rows = pl.ds(pl.multiple_of(i * 16, 16), 16)
+            normed = raw[block, rows, part].astype(jnp.float32) - stat_col[block, rows, 0:1]
+            normed = normed * stat_col[block, rows, 1:2]
+            a1[block, rows, part] = (normed * row_a[block, rows, part] + row_b[block, rows, part]).astype(
+                jnp.bfloat16
+            )
+
     qkv.ready()
-    one.ready()
 
     pieces, piece = home2.shape[0], home2.shape[2]
-    partner = at.at(z=at.zh * 2 + 1 - at.zl)
     own_rows = pl.ds(pl.multiple_of(at.zl * HD, HD), HD)
     other_rows = pl.ds(pl.multiple_of((1 - at.zl) * HD, HD), HD)
 
@@ -397,7 +411,7 @@
         swap1(h).start()
         home1[h] = acc1[own_rows, :]
 
-    proj.across()
+    proj.near()
 
     def rotate(vectors, gains):
         power = jnp.mean(vectors * vectors, axis=-1, keepdims=True)
@@ -423,8 +437,10 @@
         )
 
     two.start()
+    proj.far()
+    two.relay()
+    proj.across()
     proj.ready()
-    two.relay()
     two.ready()
 
     @pl.loop(0, pieces)
@@ -440,7 +456,7 @@
     proj.drain()
     one.drain()
     two.drain()
-    for o in (1, 2, 3):
+    for o in range(1, 8):
         stat_copy(o).wait_send()
 
     @pl.loop(0, heads)
@@ -452,7 +468,7 @@
         columns = pl.ds(pl.multiple_of(n * piece, HD), piece)
         swap2(n).wait_recv()
         projected = home2[n] + theirs2[n].astype(jnp.float32)
-        result[n] = (row_a[:, columns] * projected).astype(jnp.bfloat16)
+        result[n] = (row_gate[:, columns] * projected).astype(jnp.bfloat16)
         store(n).start()
 
     @pl.loop(0, pieces)
@@ -481,9 +497,10 @@
         scratch_shapes=[
             pltpu.VMEM((rows, wide), bf16),
             pltpu.VMEM((1, rows), jnp.int32),
+            pltpu.VMEM((1, rows), jnp.int32),
             pltpu.VMEM((1, clip_lengths.shape[0]), jnp.int32),
-            pltpu.VMEM((shift_table.shape[0], wide), f32),
-            pltpu.VMEM((shift_table.shape[0], wide), f32),
+            pltpu.VMEM((shift_table.shape[0], 2 * wide), f32),
+            pltpu.VMEM((shift_table.shape[0], 2 * wide), f32),
             pltpu.VMEM((shift_table.shape[0], wide), f32),
             pltpu.VMEM((heads * HD,), f32),
             pltpu.VMEM((heads * HD,), f32),
@@ -493,17 +510,19 @@
             pltpu.VMEM((pieces, rows, piece), bf16),
             dma((8,)),
             dma((pieces,)),
+            dma((2,)),
             pltpu.VMEM((4 * w_qkv.shape[0], w_qkv.shape[1]), bf16),
             pltpu.VMEM((4 * w_out.shape[0], w_out.shape[1]), bf16),
-            pltpu.VMEM((rows, wide), bf16),
+            pltpu.VMEM((2, rows, 2 * wide), bf16),
             pltpu.VMEM((2, rows, 2 * wide), bf16),
             pltpu.VMEM((rows, heads * HD), bf16),
             pltpu.VMEM((2, rows, 2 * heads * HD), bf16),
-            pltpu.VMEM((rows, wide), f32),
+            pltpu.VMEM((2, rows, 2 * wide), f32),
+            pltpu.VMEM((2, rows, 2 * wide), f32),
             pltpu.VMEM((rows, wide), f32),
             pltpu.VMEM((rows, HD), f32),
-            pltpu.VMEM((rows, HD), f32),
-            pltpu.VMEM((4, 8, rows), f32),
+            pltpu.VMEM((2, rows, HD), f32),
+            pltpu.VMEM((8, 8, rows), f32),
             pltpu.VMEM((heads, rows, 3 * HD), f32),
             pltpu.VMEM((heads, rows, 3 * HD), bf16),
             pltpu.VMEM((heads, rows, 3 * HD), bf16),
@@ -512,7 +531,7 @@
             pltpu.VMEM((pieces, rows, piece), bf16),
             pltpu.VMEM((2 * rows, 3 * HD), f32),
             pltpu.VMEM((2 * rows, piece), f32),
-            dma((3,)), dma((3,)),
+            dma((7,)), dma((7,)),
             dma((heads,)), dma((heads,)),
             dma((pieces,)), dma((pieces,)),
         ]

time: 92.6 us -> 81.5 us (0.88)
  the two profiles are of different devices: /device:TPU:164 before, /device:TPU:125 now
where the time goes in v3:
time: 81.5 us; the launch traced here: 81.4 us
  Pallas kernels  79.7 us (98%)
  local copies, waits for them, and re-layouts  1.72 us (2%)
    pallas_call x1, Pallas kernels, shards(): pl.pallas_call(block_kernel, out_shape=jax.ShapeDtypeStruct((rows, wide),...  79.7 us
    unnamed x1, local copies, waits for them, and re-layouts  1.72 us

profile of v3, /device:TPU:125, one launch (start us, length us, event | category | flops | bytes accessed | tf_op | source)
XLA Modules:
  0.0 81.4 jit_solution(2561164144686197850)
XLA Ops:
  0.0 79.7 %shard_map.100 = bf16[128,1280]{1,0:T(8,128)(2,1)} custom-call(bf16[128,1280]{1,0:T(8,128)(2,1)} %tokens_in.1, s32[1,128]{1,0:T(1,128)} %bitcast.2, s32[1,64]{1,0:T(1,128)} %bitcast.3, f32[16,5120]{1,0:T(8,128)} %shift_in.1, f32[16,5120]{1,0:T(8,128)} %scale_in.1, f32[16,1280]{1,0:T(8,128)} %gate_in.1, bf16[640,1920]{1,0:T(8,128)(2,1)} %wq.1, ...), custom_call_target="tpu_custom_call" | custom-call | tf_op jit(solution)/shard_map/pallas_call | solution.py:492
  79.7 1.7 %copy.12 = bf16[128,1280]{1,0:T(8,128)(2,1)} copy(bf16[128,1280]{1,0:T(8,128)(2,1)} %shard_map.100) | data formatting | bytes 655360

commit v4 on v3

--- a/solution.py
+++ b/solution.py
@@ -39,8 +39,8 @@
 
 
 class Weights:
-    def __init__(self, at, tile, buf, sems, by_columns):
-        self.at, self.tile, self.buf, self.by_columns = at, tile, buf, by_columns
+    def __init__(self, at, tile, buf, sems, by_columns, base=0):
+        self.at, self.tile, self.buf, self.by_columns, self.base = at, tile, buf, by_columns, base
         self.rows, self.cols = tile.shape
         (self.sx, self.rx, self.sf, self.rf, self.sy, self.ry, self.sc, self.rc, self.own) = sems
 
@@ -57,7 +57,7 @@
 
     def slot(self, x, quarter, core=None):
         core = self.at.core if core is None else core
-        return self.cut(self.buf, (x % 4) * self.rows, quarter % 4, core)
+        return self.cut(self.buf, self.base + (x % 4) * self.rows, quarter % 4, core)
 
     def x1(self, side, i):
         a = self.at
@@ -89,7 +89,7 @@
         return remote(ref, ref, self.sc.at[t - 1, i], self.rc.at[t - 1, i], a.at(core=1 - a.core))
 
     def local(self):
-        first = pl.multiple_of(self.at.x * self.rows, 16)
+        first = pl.multiple_of(self.base + self.at.x * self.rows, 16)
         return pltpu.make_async_copy(self.tile, self.buf.at[pl.ds(first, self.rows), :], self.own)
 
     def start(self):
@@ -239,6 +239,154 @@
         self.each(body)
 
 
+class Foreign:
+    def __init__(self, at, tile, buf, sems):
+        self.at, self.tile, self.buf = at, tile, buf
+        self.rows, self.cols = tile.shape
+        (self.sz, self.rz, self.sx, self.rx, self.sf, self.rf, self.sy, self.ry, self.sg, self.rg, self.sc, self.rc) = sems
+        self.turn = 1 - 2 * at.core
+
+    def piece(self, x, y, zl=None, whole=False):
+        zl = 1 - self.at.zl if zl is None else zl
+        count = self.rows if whole else self.rows // 4
+        first = (zl * 4 + (x + 4) % 4) * self.rows + (0 if whole else (y + 4) % 4 * count)
+        half = self.cols // 2
+        return self.buf.at[
+            pl.ds(pl.multiple_of(first, 16), count), pl.ds(pl.multiple_of(self.at.core * half, 128), half)
+        ]
+
+    def z1(self):
+        a, count, half = self.at, self.rows // 4, self.cols // 2
+        own = self.tile.at[
+            pl.ds(pl.multiple_of(a.y * count, 16), count), pl.ds(pl.multiple_of(a.core * half, 128), half)
+        ]
+        to = a.at(z=a.zh * 2 + 1 - a.zl)
+        return remote(own, self.piece(a.x, a.y, a.zl), self.sz, self.rz, to)
+
+    def x1(self, side):
+        a = self.at
+        ref = self.piece(a.x, a.y)
+        to = a.x + 1 if side == 0 else a.x + 3
+        return remote(ref, ref, self.sx.at[side], self.rx.at[side], a.at(x=to))
+
+    def x2(self):
+        a = self.at
+        ref = self.piece(a.x - self.turn, a.y)
+        return remote(ref, ref, self.sf, self.rf, a.at(x=a.x + self.turn + 4))
+
+    def y1(self, side, t):
+        a = self.at
+        ref = self.piece(a.x + t, a.y)
+        to = a.y + 1 if side == 0 else a.y + 3
+        return remote(ref, ref, self.sy.at[side, t], self.ry.at[side, t], a.at(y=to))
+
+    def y2(self, t):
+        a = self.at
+        ref = self.piece(a.x + t, a.y - self.turn)
+        return remote(ref, ref, self.sg.at[t], self.rg.at[t], a.at(y=a.y + self.turn + 4))
+
+    def c1(self, t):
+        a = self.at
+        ref = self.piece(a.x + t, 0, whole=True)
+        return remote(ref, ref, self.sc.at[t], self.rc.at[t], a.at(core=1 - a.core))
+
+    def start(self):
+        self.z1().start()
+
+    def along(self):
+        self.z1().wait_recv()
+        for side in (0, 1):
+            self.x1(side).start()
+
+    def far(self):
+        for side in (0, 1):
+            self.x1(side).wait_recv()
+        self.x2().start()
+        for t in (0, 1, 3):
+            for side in (0, 1):
+                self.y1(side, t).start()
+
+    def last(self):
+        self.x2().wait_recv()
+        for side in (0, 1):
+            self.y1(side, 2).start()
+
+    def across(self):
+        for t in (0, 1, 3, 2):
+            for side in (0, 1):
+                self.y1(side, t).wait_recv()
+            self.y2(t).start()
+
+    def share(self):
+        for t in (0, 1, 3, 2):
+            self.y2(t).wait_recv()
+            self.c1(t).start()
+
+    def ready(self):
+        for t in range(4):
+            self.c1(t).wait_recv()
+
+    def drain(self):
+        self.z1().wait_send()
+        self.x2().wait_send()
+        for side in (0, 1):
+            self.x1(side).wait_send()
+            for t in range(4):
+                self.y1(side, t).wait_send()
+        for t in range(4):
+            self.y2(t).wait_send()
+            self.c1(t).wait_send()
+
+
+class Ring:
+    def __init__(self, at, buf, sems):
+        self.at, self.buf = at, buf
+        self.half, self.width = buf.shape[0] // 2, buf.shape[1] // 4
+        self.send, self.recv, self.relay_send = sems
+
+    def view(self, place, half):
+        column = pl.multiple_of((place + 4) % 4 * self.width, 128)
+        return self.buf.at[pl.ds(half * self.half, self.half), pl.ds(column, self.width)]
+
+    def copy(self, place, half, side, send):
+        ref = self.view(place, half)
+        to = self.at.z + 2 if side == 0 else self.at.z + 6
+        return remote(ref, ref, send, self.recv.at[(place + 4) % 4, half], self.at.at(z=to))
+
+    def out(self, side, half):
+        return self.copy(self.at.zh, half, side, self.send.at[side, half])
+
+    def forward(self, side):
+        place = self.at.zh - 1 if side == 0 else self.at.zh + 1
+        return self.copy(place, side, side, self.relay_send.at[side])
+
+    def came(self, place, half):
+        ref = self.view(place, half)
+        pltpu.make_async_copy(ref, ref, self.recv.at[(place + 4) % 4, half]).wait()
+
+    def start(self):
+        for side, half in ((0, 0), (1, 1), (0, 1), (1, 0)):
+            self.out(side, half).start()
+
+    def relay(self):
+        self.came(self.at.zh - 1, 0)
+        self.forward(0).start()
+        self.came(self.at.zh + 1, 1)
+        self.forward(1).start()
+
+    def ready(self):
+        self.came(self.at.zh - 1, 1)
+        self.came(self.at.zh + 1, 0)
+        self.came(self.at.zh + 2, 0)
+        self.came(self.at.zh + 2, 1)
+
+    def drain(self):
+        for side in (0, 1):
+            for half in (0, 1):
+                self.out(side, half).wait_send()
+            self.forward(side).wait_send()
+
+
 def bucket_rows(pick, table):
     first = table.astype(jnp.bfloat16)
     rest = table - first.astype(jnp.float32)
@@ -251,12 +399,13 @@
 def block_kernel(
     tokens_in, ids_in, clips_in, shift_in, scale_in, gate_in, wq, wo, qg_in, kg_in, out,
     tokens, ids, their_ids, clips, shift, scale, gate, qg, kg, cosine, sine, mask, result, in_sem, out_sem, id_sem,
-    wq_all, wo_all, raw, a1, att, a2, row_a, row_b, row_gate, stat_in, stat_col, stats,
-    home1, mine1, theirs1, home2, mine2, theirs2, acc1, acc2,
-    stat_send, stat_recv, c1_send, c1_recv, c2_send, c2_recv,
+    wq_all, wo_all, raw, a1, a2, row_a, row_b, row_gate, stat_in, stat_col, stats,
+    home1, mine1, theirs1, acc1,
+    stat_send, stat_recv, c1_send, c1_recv,
     qs0, qs1, qs2, qs3, qs4, qs5, qs6, qs7, qs8,
     os0, os1, os2, os3, os4, os5, os6, os7, os8,
-    as0, as1, bs0, bs1,
+    as0, as1, bs0, bs1, bs2,
+    fs0, fs1, fs2, fs3, fs4, fs5, fs6, fs7, fs8, fs9, fs10, fs11,
 ):
     at = Place()
     wide = tokens.shape[1]
@@ -285,14 +434,16 @@
     pl.semaphore_wait(barrier, len(friends))
 
     qkv = Weights(at, wq, wq_all, (qs0, qs1, qs2, qs3, qs4, qs5, qs6, qs7, qs8), False)
-    proj = Weights(at, wo, wo_all, (os0, os1, os2, os3, os4, os5, os6, os7, os8), True)
+    proj = Weights(at, wo, wo_all, (os0, os1, os2, os3, os4, os5, os6, os7, os8), True, at.zl * 4 * wo.shape[0])
     one = Spread(at, tokens_in, raw, (as0, as1))
-    two = Spread(at, att, a2, (bs0, bs1))
+    two = Ring(at, a2, (bs0, bs1, bs2))
+    other = Foreign(at, wo, wo_all, (fs0, fs1, fs2, fs3, fs4, fs5, fs6, fs7, fs8, fs9, fs10, fs11))
 
     partner = at.at(z=at.zh * 2 + 1 - at.zl)
     loads[1].wait()
     id_copy = remote(ids, their_ids, id_sem.at[0], id_sem.at[1], partner)
     id_copy.start()
+    other.start()
     one.start()
     qkv.start()
     for i, load in enumerate(loads):
@@ -359,6 +510,7 @@
     qkv.far()
     proj.start()
     qkv.across()
+    other.along()
 
     for o in range(1, 8):
         stat_copy(o).wait_recv()
@@ -386,9 +538,10 @@
                 jnp.bfloat16
             )
 
+    other.far()
     qkv.ready()
 
-    pieces, piece = home2.shape[0], home2.shape[2]
+    pieces, piece = result.shape[0], result.shape[2]
     own_rows = pl.ds(pl.multiple_of(at.zl * HD, HD), HD)
     other_rows = pl.ds(pl.multiple_of((1 - at.zl) * HD, HD), HD)
 
@@ -398,9 +551,6 @@
     def store(n):
         columns = pl.ds(pl.multiple_of(n * piece, HD), piece)
         return pltpu.make_async_copy(result.at[n], out.at[:, columns], out_sem.at[n])
-
-    def swap2(h):
-        return remote(mine2.at[h], theirs2.at[h], c2_send.at[h], c2_recv.at[h], partner)
 
     @pl.loop(0, heads)
     def _(h):
@@ -412,6 +562,7 @@
         home1[h] = acc1[own_rows, :]
 
     proj.near()
+    other.last()
 
     def rotate(vectors, gains):
         power = jnp.mean(vectors * vectors, axis=-1, keepdims=True)
@@ -432,30 +583,33 @@
         ) * (1.0 / math.sqrt(HD))
         raised = jnp.where(mask[...] > 0.0, jnp.exp(scores), 0.0)
         weights = (raised / jnp.sum(raised, axis=-1, keepdims=True)).astype(jnp.bfloat16)
-        att[:, head] = jnp.dot(weights, value, preferred_element_type=jnp.float32).astype(
+        spot = pl.ds(pl.multiple_of(at.zh * (heads * HD) + h * HD, HD), HD)
+        a2[:, spot] = jnp.dot(weights, value, preferred_element_type=jnp.float32).astype(
             jnp.bfloat16
         )
 
     two.start()
     proj.far()
+    other.across()
     two.relay()
     proj.across()
+    other.share()
     proj.ready()
+    other.ready()
     two.ready()
 
     @pl.loop(0, pieces)
     def _(n):
         columns = pl.ds(pl.multiple_of(n * piece, HD), piece)
-        left = a2[...].reshape(2 * HD, a2.shape[2])
-        acc2[...] = jnp.dot(left, wo_all[:, columns], preferred_element_type=jnp.float32)
-        mine2[n] = acc2[other_rows, :].astype(jnp.bfloat16)
-        swap2(n).start()
-        home2[n] = acc2[own_rows, :]
+        projected = jnp.dot(a2[...], wo_all[:, columns], preferred_element_type=jnp.float32)
+        result[n] = (row_gate[:, columns] * projected).astype(jnp.bfloat16)
+        store(n).start()
 
     qkv.drain()
     proj.drain()
     one.drain()
     two.drain()
+    other.drain()
     for o in range(1, 8):
         stat_copy(o).wait_send()
 
@@ -465,15 +619,6 @@
 
     @pl.loop(0, pieces)
     def _(n):
-        columns = pl.ds(pl.multiple_of(n * piece, HD), piece)
-        swap2(n).wait_recv()
-        projected = home2[n] + theirs2[n].astype(jnp.float32)
-        result[n] = (row_gate[:, columns] * projected).astype(jnp.bfloat16)
-        store(n).start()
-
-    @pl.loop(0, pieces)
-    def _(n):
-        swap2(n).wait_send()
         store(n).wait()
 
 
@@ -487,6 +632,8 @@
     bf16, f32 = jnp.bfloat16, jnp.float32
     dma = pltpu.SemaphoreType.DMA
     weight_sems = [dma((2, 2)), dma((2, 2)), dma((2,)), dma((2,)), dma((3, 2)), dma((3, 2)), dma((3, 4)), dma((3, 4)), dma]
+    ring_sems = [dma((2, 2)), dma((4, 2)), dma((2,))]
+    foreign_sems = [dma, dma, dma((2,)), dma((2,)), dma, dma, dma((2, 4)), dma((2, 4))] + [dma((4,))] * 4
     spread_sems = [dma((10,)), dma((4, 2))]
     hbm = pl.BlockSpec(memory_space=pltpu.HBM)
     return pl.pallas_call(
@@ -512,11 +659,10 @@
             dma((pieces,)),
             dma((2,)),
             pltpu.VMEM((4 * w_qkv.shape[0], w_qkv.shape[1]), bf16),
-            pltpu.VMEM((4 * w_out.shape[0], w_out.shape[1]), bf16),
+            pltpu.VMEM((8 * w_out.shape[0], w_out.shape[1]), bf16),
             pltpu.VMEM((2, rows, 2 * wide), bf16),
             pltpu.VMEM((2, rows, 2 * wide), bf16),
-            pltpu.VMEM((rows, heads * HD), bf16),
-            pltpu.VMEM((2, rows, 2 * heads * HD), bf16),
+            pltpu.VMEM((rows, 4 * heads * HD), bf16),
             pltpu.VMEM((2, rows, 2 * wide), f32),
             pltpu.VMEM((2, rows, 2 * wide), f32),
             pltpu.VMEM((rows, wide), f32),
@@ -526,16 +672,11 @@
             pltpu.VMEM((heads, rows, 3 * HD), f32),
             pltpu.VMEM((heads, rows, 3 * HD), bf16),
             pltpu.VMEM((heads, rows, 3 * HD), bf16),
-            pltpu.VMEM((pieces, rows, piece), f32),
-            pltpu.VMEM((pieces, rows, piece), bf16),
-            pltpu.VMEM((pieces, rows, piece), bf16),
             pltpu.VMEM((2 * rows, 3 * HD), f32),
-            pltpu.VMEM((2 * rows, piece), f32),
             dma((7,)), dma((7,)),
             dma((heads,)), dma((heads,)),
-            dma((pieces,)), dma((pieces,)),
         ]
-        + weight_sems + weight_sems + spread_sems + spread_sems,
+        + weight_sems + weight_sems + spread_sems + ring_sems + foreign_sems,
         compiler_params=pltpu.CompilerParams(
             collective_id=0, has_side_effects=True, vmem_limit_bytes=60 * 1024 * 1024
         ),

time: 81.5 us -> 78 us (0.957)
  the two profiles are of different devices: /device:TPU:125 before, /device:TPU:51 now
where the time goes in v4:
time: 78 us; the launch traced here: 77.9 us
  Pallas kernels  76.1 us (98%)
  local copies, waits for them, and re-layouts  1.72 us (2%)
    pallas_call x1, Pallas kernels, shards(): pl.pallas_call(block_kernel, out_shape=jax.ShapeDtypeStruct((rows, wide),...  76.1 us
    unnamed x1, local copies, waits for them, and re-layouts  1.72 us

profile of v4, /device:TPU:51, one launch (start us, length us, event | category | flops | bytes accessed | tf_op | source)
XLA Modules:
  0.0 77.9 jit_solution(6768658817684068056)
XLA Ops:
  0.0 76.1 %shard_map.100 = bf16[128,1280]{1,0:T(8,128)(2,1)} custom-call(bf16[128,1280]{1,0:T(8,128)(2,1)} %tokens_in.1, s32[1,128]{1,0:T(1,128)} %bitcast.2, s32[1,64]{1,0:T(1,128)} %bitcast.3, f32[16,5120]{1,0:T(8,128)} %shift_in.1, f32[16,5120]{1,0:T(8,128)} %scale_in.1, f32[16,1280]{1,0:T(8,128)} %gate_in.1, bf16[640,1920]{1,0:T(8,128)(2,1)} %wq.1, ...), custom_call_target="tpu_custom_call" | custom-call | tf_op jit(solution)/shard_map/pallas_call | solution.py:639
  76.2 1.7 %copy.12 = bf16[128,1280]{1,0:T(8,128)(2,1)} copy(bf16[128,1280]{1,0:T(8,128)(2,1)} %shard_map.100) | data formatting | bytes 655360

commit v5 on v4

--- a/solution.py
+++ b/solution.py
@@ -116,8 +116,8 @@
             self.y1(2, side).start()
             self.c1(2, side).start()
 
-    def across(self):
-        for t in (3, 1, 2):
+    def across(self, tiles=(3, 1, 2)):
+        for t in tiles:
             for side in (0, 1):
                 self.y1(t, side).wait_recv()
                 self.c1(t, 3 if side == 0 else 2).start()
@@ -473,7 +473,7 @@
         stat_copy(o).start()
 
     qkv.near()
-    one.relay()
+    one.relay((0,))
     count = clips.shape[1]
     lengths = jnp.broadcast_to(clips[...], (8, count)).astype(jnp.bfloat16)
     before = (
@@ -508,10 +508,9 @@
     row_b[1 - at.zl] = bucket_rows_of(their_ids, shift)
 
     qkv.far()
+    one.relay((1, 2))
     proj.start()
-    qkv.across()
-    other.along()
-
+    qkv.across((3, 1))
     for o in range(1, 8):
         stat_copy(o).wait_recv()
 
@@ -525,6 +524,8 @@
         rstd = lax.rsqrt(total * (1.0 / (4 * wide)) + EPS)
         stat_col[block] = jnp.where(index == 0, mean, jnp.where(index == 1, rstd, 0.0)).T
 
+    qkv.across((2,))
+    other.along()
     for slot in range(4):
         one.ready((slot,))
         block, part = slot % 2, pl.ds(slot // 2 * wide, wide)
@@ -538,8 +539,8 @@
                 jnp.bfloat16
             )
 
+    qkv.ready()
     other.far()
-    qkv.ready()
 
     pieces, piece = result.shape[0], result.shape[2]
     own_rows = pl.ds(pl.multiple_of(at.zl * HD, HD), HD)

time: 78 us -> 76.2 us (0.977)
  the two profiles are of different devices: /device:TPU:51 before, /device:TPU:24 now
where the time goes in v5:
time: 76.2 us; the launch traced here: 76.1 us
  Pallas kernels  74.3 us (98%)
  local copies, waits for them, and re-layouts  1.72 us (2%)
    pallas_call x1, Pallas kernels, shards(): pl.pallas_call(block_kernel, out_shape=jax.ShapeDtypeStruct((rows, wide),...  74.3 us
    unnamed x1, local copies, waits for them, and re-layouts  1.72 us

profile of v5, /device:TPU:24, one launch (start us, length us, event | category | flops | bytes accessed | tf_op | source)
XLA Modules:
  0.0 76.1 jit_solution(10232273531854853688)
XLA Ops:
  0.0 74.3 %shard_map.100 = bf16[128,1280]{1,0:T(8,128)(2,1)} custom-call(bf16[128,1280]{1,0:T(8,128)(2,1)} %tokens_in.1, s32[1,128]{1,0:T(1,128)} %bitcast.2, s32[1,64]{1,0:T(1,128)} %bitcast.3, f32[16,5120]{1,0:T(8,128)} %shift_in.1, f32[16,5120]{1,0:T(8,128)} %scale_in.1, f32[16,1280]{1,0:T(8,128)} %gate_in.1, bf16[640,1920]{1,0:T(8,128)(2,1)} %wq.1, ...), custom_call_target="tpu_custom_call" | custom-call | tf_op jit(solution)/shard_map/pallas_call | solution.py:640
  74.4 1.7 %copy.12 = bf16[128,1280]{1,0:T(8,128)(2,1)} copy(bf16[128,1280]{1,0:T(8,128)(2,1)} %shard_map.100) | data formatting | bytes 655360

commit v6 on v5

--- a/solution.py
+++ b/solution.py
@@ -556,11 +556,15 @@
     @pl.loop(0, heads)
     def _(h):
         columns = pl.ds(pl.multiple_of(h * (3 * HD), HD), 3 * HD)
-        left = a1[...].reshape(2 * HD, a1.shape[2])
-        acc1[...] = jnp.dot(left, wq_all[:, columns], preferred_element_type=jnp.float32)
-        mine1[h] = acc1[other_rows, :].astype(jnp.bfloat16)
+        mine1[h] = jnp.dot(
+            a1[1 - at.zl], wq_all[:, columns], preferred_element_type=jnp.float32
+        ).astype(jnp.bfloat16)
         swap1(h).start()
-        home1[h] = acc1[own_rows, :]
+
+    @pl.loop(0, heads)
+    def _(h):
+        columns = pl.ds(pl.multiple_of(h * (3 * HD), HD), 3 * HD)
+        home1[h] = jnp.dot(a1[at.zl], wq_all[:, columns], preferred_element_type=jnp.float32)
 
     proj.near()
     other.last()

time: 76.2 us -> 76 us (level)
  no operation moved by 1% of the time
where the time goes in v6:
time: 76 us; the launch traced here: 75.9 us
  Pallas kernels  74.2 us (98%)
  local copies, waits for them, and re-layouts  1.72 us (2%)
    pallas_call x1, Pallas kernels, shards(): pl.pallas_call(block_kernel, out_shape=jax.ShapeDtypeStruct((rows, wide),...  74.2 us
    unnamed x1, local copies, waits for them, and re-layouts  1.72 us

profile of v6, /device:TPU:24, one launch (start us, length us, event | category | flops | bytes accessed | tf_op | source)
XLA Modules:
  0.0 75.9 jit_solution(16444951015355207210)
XLA Ops:
  0.0 74.2 %shard_map.100 = bf16[128,1280]{1,0:T(8,128)(2,1)} custom-call(bf16[128,1280]{1,0:T(8,128)(2,1)} %tokens_in.1, s32[1,128]{1,0:T(1,128)} %bitcast.2, s32[1,64]{1,0:T(1,128)} %bitcast.3, f32[16,5120]{1,0:T(8,128)} %shift_in.1, f32[16,5120]{1,0:T(8,128)} %scale_in.1, f32[16,1280]{1,0:T(8,128)} %gate_in.1, bf16[640,1920]{1,0:T(8,128)(2,1)} %wq.1, ...), custom_call_target="tpu_custom_call" | custom-call | tf_op jit(solution)/shard_map/pallas_call | solution.py:644
  74.2 1.7 %copy.12 = bf16[128,1280]{1,0:T(8,128)(2,1)} copy(bf16[128,1280]{1,0:T(8,128)(2,1)} %shard_map.100) | data formatting | bytes 655360
